TPU v7x, 32 devices: a whole 2x2x4 slice. The times are simulated.
32 devices in a mesh: prow: 8 (over y, x, core), pcol: 4 (over z).
Axes of the slice: x: 2, y: 2, z: 4, core: 2. Of those that a mesh axis runs over, the one named last changes fastest.
Arguments:
- inverse_block: float32 [3, 8, 256, 6, 4, 256], P(None, 'prow', None, None, 'pcol'), as said below
- panel_first: float32 [3, 8, 256, 512], P(None, 'prow', 'pcol'), may hold values from -0.078125 to 0.078125
- panel_second: float32 [3, 8, 256, 512], P(None, 'prow', 'pcol'), may hold values from -0.078125 to 0.078125
- diag_first: float32 [512, 512], replicated, may hold values from -6 to 6
- diag_second: float32 [512, 512], replicated, may hold values from -6 to 6
- pattern_first: int32 [24], replicated, may hold values from 0 to 1, as said below
- pattern_second: int32 [24], replicated, may hold values from 0 to 1, as said below
Outputs:
- column_first: float32 [3, 8, 256, 512], P(None, 'prow', 'pcol')
- column_second: float32 [3, 8, 256, 512], P(None, 'prow', 'pcol')
- diagonal_first: float32 [512, 512], replicated
- diagonal_second: float32 [512, 512], replicated
Inputs may be any that keep to these rules, and one draw needn't show every extreme that they name: inverse_block is symmetric as a matrix of 6144 rows: its entry (i, j) equals its entry (j, i) exactly. `pattern_first`: at least one entry is 1. `pattern_second`: at least one entry is 1.
All inputs are finite; a program needn't handle non-finite values.
Results may differ from a plain program's by a relative error of at most 0.000071.
Values sent between devices are 32-bit elements; how exact they have to be, the bound alone decides.
A program may use at most 64 MiB of HBM per device.

v0:
```python
import jax
import jax.numpy as jnp
from jax import lax
from jax.sharding import PartitionSpec as P


def from_root(block, axis, owner):
    block = jnp.where(lax.axis_index(axis) == owner, block, jnp.zeros_like(block))
    return lax.psum(block, axis)


def body(
    inverse_block, panel_first, panel_second, diag_first, diag_second, pattern_first, pattern_second
):
    row_count = lax.axis_size("prow")
    col_count = lax.axis_size("pcol")
    factor = row_count // col_count
    row_index = lax.axis_index("prow")
    col_index = lax.axis_index("pcol")
    row_blocks = inverse_block.shape[0]
    block_rows = inverse_block.shape[2]
    col_blocks = inverse_block.shape[3]
    matrix = inverse_block.reshape(row_blocks, block_rows, col_blocks, block_rows)
    slice_rows = panel_first.shape[2]
    col_width = panel_first.shape[3]
    highest = lax.Precision.HIGHEST

    def one_column(panel_part, pattern):
        kept_rows = lax.dynamic_index_in_dim(
            pattern.reshape(row_blocks, row_count), row_index, 1, False
        ).astype(jnp.float32)
        masked = panel_part[:, 0] * kept_rows[:, None, None]
        whole = lax.all_gather(masked, "pcol", axis=1, tiled=True)
        partial_value = jnp.einsum(
            "lsmt,lsw->mtw", matrix, whole, precision=highest, preferred_element_type=jnp.float32
        )
        totals = lax.psum(partial_value, "prow")
        chosen = lax.dynamic_index_in_dim(
            totals.reshape(row_blocks, factor, block_rows, col_width),
            row_index // col_count,
            1,
            False,
        )
        row_full = from_root(chosen, "pcol", row_index % col_count)
        result = -lax.dynamic_slice_in_dim(row_full, col_index * slice_rows, slice_rows, 1)
        result = result * kept_rows[:, None, None]
        partial_diag = jnp.einsum(
            "lsw,lsv->wv", masked, result, precision=highest, preferred_element_type=jnp.float32
        )
        return (result, partial_diag)

    first_col, first_part = one_column(panel_first, pattern_first)
    second_col, second_part = one_column(panel_second, pattern_second)
    first_sum, second_sum = lax.psum((first_part, second_part), ("prow", "pcol"))
    return (
        first_col[:, None],
        second_col[:, None],
        diag_first - first_sum,
        diag_second - second_sum,
    )


def solution(mesh):
    placed = (
        P(None, "prow", None, None, "pcol", None),
        P(None, "prow", "pcol", None),
        P(None, "prow", "pcol", None),
        P(),
        P(),
        P(),
        P(),
    )
    return jax.shard_map(
        body,
        mesh=mesh,
        in_specs=placed,
        out_specs=(P(None, "prow", "pcol", None), P(None, "prow", "pcol", None), P(), P()),
        check_vma=False,
    )
```

profile of v0, /device:TPU:0, one launch (start us, length us, event | category | flops | bytes accessed | tf_op | source)
XLA Modules:
  0.0 480.3 jit_solution(14182931832954799744)
XLA Ops:
  7.2 0.0 all-gather.3.cloned.1.call-start
  7.2 0.7 reshape.41
  8.0 0.2 convert_reduce_fusion.1
  8.1 1.9 bitcast_multiply_fusion.1
  10.0 0.0 all-gather.3.cloned.1.call-update
  10.0 0.0 all-gather.5.cloned.1.call-start
  10.1 0.7 reshape.44
  10.8 0.2 convert_reduce_fusion
  11.0 1.9 bitcast_multiply_fusion
  12.9 0.0 all-gather.5.cloned.1.call-update
  12.9 0.0 all-reduce.9.cloned.1.call-start
  12.9 37.0 %all-gather.3.cloned.1.call-done = f32[3,256,512]{2,1,0:T(8,128)} async-done(((f32[3,64,512]{2,1,0:T(8,128)}), f32[3,256,512]{2,1,0:T(8,128)}) %all-gather.3.cloned.1.call-update) | async-done | bytes 1572880 | tf_op jit(solution)/shard_map/all_gather | solution.py:33
  50.0 10.4 %fusion.2 = f32[512,6,256,1]{2,0,3,1:T(8,128)S(1)} fusion(f32[3,1,256,6,1,256]{5,4,3,2,1,0:T(1,128)} %param.7, f32[3,256,512]{2,1,0:T(8,128)} %all-gather.3.cloned.1.call-done), kind=kOutput, calls=%fused_computation.2 | convolution fusion | flops 7247757312 | bytes 9437184 | tf_op jit(solution)/shard_map/lsmt,lsw->mtw/dot_general | solution.py:34
  60.4 2.4 copy.18
  62.8 25.3 %all-gather.5.cloned.1.call-done = f32[3,256,512]{2,1,0:T(8,128)} async-done(((f32[3,64,512]{2,1,0:T(8,128)}), f32[3,256,512]{2,1,0:T(8,128)}) %all-gather.5.cloned.1.call-update) | async-done | bytes 1572880 | tf_op jit(solution)/shard_map/all_gather | solution.py:33
  88.1 10.4 %fusion = f32[512,6,256,1]{2,0,3,1:T(8,128)S(1)} fusion(f32[3,1,256,6,1,256]{5,4,3,2,1,0:T(1,128)} %param.7, f32[3,256,512]{2,1,0:T(8,128)} %all-gather.5.cloned.1.call-done), kind=kOutput, calls=%fused_computation | convolution fusion | flops 7247757312 | bytes 9437184 | tf_op jit(solution)/shard_map/lsmt,lsw->mtw/dot_general | solution.py:34
  98.5 2.3 copy.21
  100.9 0.0 all-reduce.9.cloned.1.call-update
  100.9 0.0 all-reduce.11.cloned.1.call-start
  101.0 103.3 %all-reduce.9.cloned.1.call-done = (f32[3,2,256,512]{3,2,0,1:T(8,128)}, f32[3,2,256,512]{3,2,0,1:T(8,128)}) async-done(((f32[3,2,256,512]{3,2,0,1:T(8,128)}, f32[3,2,256,512]{3,2,0,1:T(8,128)}), (f32[3,2,256,512]{3,2,0,1:T(8,128)}, f32[3,2,256,512]{3,2,0,1:T(8,128)})) %all-reduce.9.cloned.1.call-update) | async-done | bytes 6291472 | tf_op jit(solution)/shard_map/psum | solution.py:37
  204.3 4.2 select_bitcast_fusion
  208.5 0.0 all-reduce.11.cloned.1.call-update
  208.5 0.2 all-reduce.7.cloned.1.call-start
  208.8 121.5 %all-reduce.11.cloned.1.call-done = (f32[3,256,512]{2,1,0:T(8,128)}, f32[3,256,512]{2,1,0:T(8,128)}) async-done(((f32[3,256,512]{2,1,0:T(8,128)}, f32[3,256,512]{2,1,0:T(8,128)}), (f32[3,256,512]{2,1,0:T(8,128)}, f32[3,256,512]{2,1,0:T(8,128)})) %all-reduce.11.cloned.1.call-update) | async-done | bytes 3145744 | tf_op jit(solution)/shard_map/psum | solution.py:9
  330.2 3.2 convolution_bitcast_fusion.1
  333.4 3.2 convolution_bitcast_fusion
  336.5 0.0 all-reduce.7.cloned.1.call-update
  336.6 1.9 fusion.8
  338.5 1.9 fusion.9
  340.4 129.7 %all-reduce.7.cloned.1.call-done = (f32[512,512]{1,0:T(8,128)}, f32[512,512]{1,0:T(8,128)}) async-done(((f32[512,512]{1,0:T(8,128)}, f32[512,512]{1,0:T(8,128)}), (f32[512,512]{1,0:T(8,128)}, f32[512,512]{1,0:T(8,128)})) %all-reduce.7.cloned.1.call-update) | async-done | bytes 2097168 | tf_op jit(solution)/shard_map/psum | solution.py:54
  470.1 2.5 sub.12
  472.6 1.2 sub.13
  (10 shorter events, 0.0 us)
Async XLA Ops:
  7.2 42.8 %all-gather.3.cloned.1.call-start = ((), (), s32[]{:S(2)}) async-start(), calls=%async_computation | async-start | bytes 1966080 | tf_op jit(solution)/shard_map/all_gather | solution.py:33
  10.0 78.1 %all-gather.5.cloned.1.call-start = ((), (), s32[]{:S(2)}) async-start(), calls=%async_computation.1 | async-start | bytes 1966080 | tf_op jit(solution)/shard_map/all_gather | solution.py:33
  12.9 191.4 %all-reduce.9.cloned.1.call-start = ((), (), s32[]{:S(2)}) async-start(), calls=%async_computation.3 | async-start | bytes 12582912 | tf_op jit(solution)/shard_map/psum | solution.py:37
  100.9 229.3 %all-reduce.11.cloned.1.call-start = ((), (), s32[]{:S(2)}) async-start(), calls=%async_computation.4 | async-start | bytes 6291456 | tf_op jit(solution)/shard_map/psum | solution.py:9
  208.5 121.7 %copy-start = (f32[3,1,64,512]{3,2,1,0:T(8,128)S(1)}, f32[3,1,64,512]{3,2,1,0:T(8,128)}, u32[]{:S(2)}) copy-start(f32[3,1,64,512]{3,2,1,0:T(8,128)} %param.8) | copy-start | bytes 1179652
  208.5 124.9 %copy-start.1 = (f32[3,1,64,512]{3,2,1,0:T(8,128)S(1)}, f32[3,1,64,512]{3,2,1,0:T(8,128)}, u32[]{:S(2)}) copy-start(f32[3,1,64,512]{3,2,1,0:T(8,128)} %param.9) | copy-start | bytes 1179652
  208.5 261.5 %all-reduce.7.cloned.1.call-start = ((), (), s32[]{:S(2)}) async-start(), calls=%async_computation.2 | async-start | bytes 4194304 | tf_op jit(solution)/shard_map/psum | solution.py:54
  336.5 133.5 %copy-start.2 = (f32[512,512]{1,0:T(8,128)S(1)}, f32[512,512]{1,0:T(8,128)}, u32[]{:S(2)}) copy-start(f32[512,512]{1,0:T(8,128)} %param.10) | copy-start | bytes 3145732
  470.1 2.6 copy-start.3
  470.1 2.6 copy-start.4
Sparse Core Ops, SparseCore 0:
  10.1 39.7 all-gather.2
  52.1 35.9 all-gather.4
  101.0 103.2 all-reduce.8
  208.6 121.5 all-reduce.10
  337.1 132.9 all-reduce.6
where the time goes:
time: 481 us; the launch traced here: 480 us
  waiting for transfers between devices  417 us (87%)
  matrix products  27.1 us (6%)
  other arithmetic  15.8 us (3%)
  between operations  13.8 us (3%)
  local copies, waits for them, and re-layouts  6.27 us (1%)
    psum x1, waiting for transfers between devices, body(): lax.psum((first_part, second_part), ('prow', 'pcol'))  130 us
    psum x1, waiting for transfers between devices, from_root(): return lax.psum(block, axis)  121 us
    psum x1, waiting for transfers between devices, one_column(): totals = lax.psum(partial_value, 'prow')  103 us
    all_gather x2, waiting for transfers between devices, one_column(): whole = lax.all_gather(masked, 'pcol', axis=1, tiled=True)  62.3 us
    dot_general x2, matrix products, one_column(): jnp.einsum('lsmt,lsw->mtw', matrix, whole, precision=highest, preferred_e...  20.8 us
  transfers between devices with their start and end apart: 5, of which 5 were waited for; matrix products, arithmetic and copies ran while one was open for 4% of the time, Pallas kernels for 0%

commit v1 on v0

v1 whole, which is shorter than its diff:
```python
import functools

import jax
import jax.numpy as jnp
from jax import lax
from jax.experimental import pallas as pl
from jax.experimental.pallas import tpu as pltpu
from jax.sharding import PartitionSpec as P

MESH = pl.DeviceIdType.MESH
LANES = 128
F32 = jnp.float32
BF16 = jnp.bfloat16


def halves(value):
    high = value.astype(BF16)
    return high, (value - high.astype(F32)).astype(BF16)


def dot3(left, right, dims):
    def one(a, b):
        return lax.dot_general(a, b, (dims, ((), ())), preferred_element_type=F32)

    return one(left[0], right[0]) + (one(left[0], right[1]) + one(left[1], right[0]))


def kernel(
    sizes,
    mat,
    p0,
    p1,
    pat0,
    pat1,
    col0,
    col1,
    dia0,
    dia1,
    xbuf,
    ahi,
    alo,
    xhi,
    xlo,
    ybuf,
    rsbuf,
    khi,
    klo,
    chi,
    clo,
    dpart,
    drecv,
    dsum,
    zbuf,
    s1_send,
    s1_recv,
    ag_send,
    ag_recv,
    sib_send,
    sib_recv,
    rs_send,
    rs_recv,
    dr_send,
    dr_recv,
    dz_send,
    dz_recv,
    da_send,
    da_recv,
):
    R, C, L, B, S, W = sizes
    F = R // C
    lane_parts = W // LANES
    RC = R // lane_parts
    r = lax.axis_index("prow")
    c = lax.axis_index("pcol")
    panels, pats, cols, dias = (p0, p1), (pat0, pat1), (col0, col1), (dia0, dia1)
    total = R * C
    me = r * C + c
    sibling = r + 1 - 2 * lax.rem(r, 2)

    barrier = pltpu.get_barrier_semaphore()

    @pl.loop(1, total)
    def _(i):
        other = lax.rem(me + i, total)
        pl.semaphore_signal(
            barrier, inc=1, device_id=(lax.div(other, C), lax.rem(other, C)), device_id_type=MESH
        )

    pl.semaphore_wait(barrier, total - 1)

    def row_part(k):
        return lax.div(k, lane_parts)

    def lanes(k):
        return pl.ds(pl.multiple_of(lax.rem(k, lane_parts) * LANES, LANES), LANES)

    def remote(src, dst, send, recv, row, column):
        return pltpu.make_async_remote_copy(
            src_ref=src,
            dst_ref=dst,
            send_sem=send,
            recv_sem=recv,
            device_id=(row, column),
            device_id_type=MESH,
        )

    plane = lax.rem(r, C)
    source = lax.div(r, C) * C + c
    own_plane = plane == c

    def first_copy(n, d):
        k = lax.rem(r + d, R)
        src = panels[n].at[:, row_part(k), :, lanes(k)]
        dst = xbuf.at[n, :, source, row_part(k), :, lanes(k)]
        return remote(src, dst, s1_send.at[n, d], s1_recv.at[n, source], k, plane)

    def first_local(n):
        src = panels[n].at[:, row_part(r), :, lanes(r)]
        dst = xbuf.at[n, :, source, row_part(r), :, lanes(r)]
        return pltpu.make_async_copy(src, dst, s1_recv.at[n, source])

    def first_wait(n, q):
        part = xbuf.at[n, :, q, row_part(r), :, lanes(r)]
        pltpu.make_async_copy(part, part, s1_recv.at[n, q]).wait()

    def strip(n, k):
        return xbuf.at[n, :, :, row_part(k), :, lanes(k)]

    def gather_copy(n, j):
        part = strip(n, r)
        return remote(
            part, part, ag_send.at[n, j], ag_recv.at[n, j], lax.rem(r + 2 * j, R), c
        )

    def gather_wait(n, j):
        part = strip(n, lax.rem(r + R - 2 * j, R))
        pltpu.make_async_copy(part, part, ag_recv.at[n, j]).wait()

    def sibling_copy(n, j):
        part = strip(n, lax.rem(r + R - 2 * j, R))
        return remote(part, part, sib_send.at[n, j], sib_recv.at[n, j], sibling, c)

    def sibling_wait(n, j):
        part = strip(n, lax.rem(sibling + R - 2 * j, R))
        pltpu.make_async_copy(part, part, sib_recv.at[n, j]).wait()

    def scatter_copy(n, d):
        z = lax.rem(c + d, C)
        return remote(
            ybuf.at[n, :, pl.ds(pl.multiple_of(z * S, S), S), :],
            rsbuf.at[n, d],
            rs_send.at[n, d],
            rs_recv.at[n, d],
            r,
            z,
        )

    def diag_row_copy(n, d):
        k = lax.rem(r + d, R)
        return remote(
            dpart.at[n, k], drecv.at[n, d], dr_send.at[n, d], dr_recv.at[n, d], k, c
        )

    def diag_col_copy(n, d):
        return remote(
            dsum.at[n], zbuf.at[n, d], dz_send.at[n, d], dz_recv.at[n, d], r, lax.rem(c + d, C)
        )

    def diag_all_copy(n, d):
        return remote(
            dias[n].at[r], dias[n].at[r], da_send.at[n, d], da_recv.at[n, d], lax.rem(r + d, R), c
        )

    def diag_all_wait(n, d):
        part = dias[n].at[lax.rem(r + R - d, R)]
        pltpu.make_async_copy(part, part, da_recv.at[n, d]).wait()

    def start_first(n):
        for d in range(1, R):
            first_copy(n, d).start()

        @pl.when(own_plane)
        def _():
            first_local(n).start()

        @pl.when(jnp.logical_not(own_plane))
        def _():
            first_copy(n, 0).start()

    def start_gather(n):
        for q in range(F * C):
            first_wait(n, q)
        for j in range(1, R // 2):
            gather_copy(n, j).start()
        sibling_copy(n, 0).start()

    def forward(n):
        for j in range(1, R // 2):
            gather_wait(n, j)
            sibling_copy(n, j).start()

    def multiply(n):
        for j in range(R // 2):
            sibling_wait(n, j)

        @pl.loop(0, L * F * C)
        def _(i):
            l = lax.div(i, F * C)
            q = lax.rem(i, F * C)
            kept = pats[n][l * R + lax.div(q, C) * C + c].astype(F32)
            rows = pl.ds(pl.multiple_of(i * S, S), S)
            high, low = halves(xbuf[n, l, q].reshape(S, W) * kept)
            xhi[rows, :] = high
            xlo[rows, :] = low

        @pl.loop(0, L)
        def _(l):
            rows = pl.ds(pl.multiple_of(l * B, B), B)
            ybuf[n, l] = dot3(
                (ahi[rows, :], alo[rows, :]), (xhi[...], xlo[...]), ((1,), (0,))
            )

        for d in range(1, C):
            scatter_copy(n, d).start()

    def finish_column(n):
        for d in range(1, C):
            scatter_copy(n, d).wait_recv()
        for l in range(L):
            kept = pats[n][l * R + r].astype(F32)
            value = ybuf[n, l, pl.ds(pl.multiple_of(c * S, S), S), :]
            for d in range(1, C):
                value = value + rsbuf[n, d, l]
            value = -(value * kept)
            cols[n][l] = value
            rows = slice(l * S, (l + 1) * S)
            chi[rows, :], clo[rows, :] = halves(value)
            khi[rows, :], klo[rows, :] = halves(panels[n][l].reshape(S, W) * kept)
        part = dot3((khi[...], klo[...]), (chi[...], clo[...]), ((0,), (0,)))
        dpart[n] = part.reshape(R, W // R, W)
        for d in range(1, R):
            diag_row_copy(n, d).start()

    def diag_rows(n):
        value = dpart[n, r]
        for d in range(1, R):
            diag_row_copy(n, d).wait_recv()
            value = value + drecv[n, d]
        dsum[n] = value
        for d in range(1, C):
            diag_col_copy(n, d).start()

    def diag_cols(n):
        value = dsum[n]
        for d in range(1, C):
            diag_col_copy(n, d).wait_recv()
            value = value + zbuf[n, d]
        dias[n][r] = value
        for d in range(1, R):
            diag_all_copy(n, d).start()

    start_first(0)
    start_first(1)

    tile = min(B, 64)

    @pl.loop(0, L * B // tile)
    def _(i):
        rows = pl.ds(pl.multiple_of(i * tile, tile), tile)
        ahi[rows, :], alo[rows, :] = halves(mat[rows, :])

    start_gather(0)
    forward(0)
    start_gather(1)
    multiply(0)
    forward(1)
    multiply(1)
    finish_column(0)
    diag_rows(0)
    finish_column(1)
    diag_cols(0)
    diag_rows(1)
    diag_cols(1)
    for n in range(2):
        for d in range(1, R):
            diag_all_wait(n, d)
        for d in range(1, R):
            first_copy(n, d).wait_send()
            diag_row_copy(n, d).wait_send()
            diag_all_copy(n, d).wait_send()

        @pl.when(jnp.logical_not(own_plane))
        def _():
            first_copy(n, 0).wait_send()

        for j in range(R // 2):
            if j > 0:
                gather_copy(n, j).wait_send()
            sibling_copy(n, j).wait_send()
        for d in range(1, C):
            scatter_copy(n, d).wait_send()
            diag_col_copy(n, d).wait_send()


def body(R, C, inverse, first, second, diag_first, diag_second, pat_first, pat_second):
    L, _, B, M, _, _ = inverse.shape
    S, W = first.shape[2:]
    F = R // C
    RC = R // (W // LANES)
    matrix = inverse.reshape(L * B, M * B)
    panels = [p.reshape(L, RC, S // RC, W) for p in (first, second)]
    vmem = pl.BlockSpec(memory_space=pltpu.VMEM)
    smem = pl.BlockSpec(memory_space=pltpu.SMEM)
    dma = pltpu.SemaphoreType.DMA
    part = W // R
    flops = 3 * 2 * L * B * M * B * 2 * W
    col0, col1, sum0, sum1 = pl.pallas_call(
        functools.partial(kernel, (R, C, L, B, S, W)),
        out_shape=[jax.ShapeDtypeStruct((L, S, W), F32)] * 2
        + [jax.ShapeDtypeStruct((R, part, W), F32)] * 2,
        in_specs=[vmem] * 3 + [smem] * 2,
        out_specs=[vmem] * 4,
        scratch_shapes=[
            pltpu.VMEM((2, L, F * C, RC, S // RC, W), F32),
            pltpu.VMEM((L * B, M * B), BF16),
            pltpu.VMEM((L * B, M * B), BF16),
            pltpu.VMEM((M * B, W), BF16),
            pltpu.VMEM((M * B, W), BF16),
            pltpu.VMEM((2, L, B, W), F32),
            pltpu.VMEM((2, C, L, S, W), F32),
            pltpu.VMEM((L * S, W), BF16),
            pltpu.VMEM((L * S, W), BF16),
            pltpu.VMEM((L * S, W), BF16),
            pltpu.VMEM((L * S, W), BF16),
            pltpu.VMEM((2, R, part, W), F32),
            pltpu.VMEM((2, R, part, W), F32),
            pltpu.VMEM((2, part, W), F32),
            pltpu.VMEM((2, C, part, W), F32),
            dma((2, R)),
            dma((2, F * C)),
            dma((2, R // 2)),
            dma((2, R // 2)),
            dma((2, R // 2)),
            dma((2, R // 2)),
            dma((2, C)),
            dma((2, C)),
            dma((2, R)),
            dma((2, R)),
            dma((2, C)),
            dma((2, C)),
            dma((2, R)),
            dma((2, R)),
        ],
        compiler_params=pltpu.CompilerParams(
            collective_id=0, has_side_effects=True, vmem_limit_bytes=56 * 1024 * 1024
        ),
        cost_estimate=pl.CostEstimate(
            flops=flops, bytes_accessed=4 * L * B * M * B, transcendentals=0
        ),
    )(matrix, *panels, pat_first, pat_second)
    return (
        col0[:, None],
        col1[:, None],
        diag_first - sum0.reshape(W, W),
        diag_second - sum1.reshape(W, W),
    )


def solution(mesh):
    placed = (
        P(None, "prow", None, None, "pcol", None),
        P(None, "prow", "pcol", None),
        P(None, "prow", "pcol", None),
        P(),
        P(),
        P(),
        P(),
    )
    return jax.shard_map(
        functools.partial(body, mesh.shape["prow"], mesh.shape["pcol"]),
        mesh=mesh,
        in_specs=placed,
        out_specs=(P(None, "prow", "pcol", None), P(None, "prow", "pcol", None), P(), P()),
        check_vma=False,
    )
```

time: 481 us -> 216 us (0.45)
  waiting for transfers between devices: 417 us -> 0 us
  Pallas kernels: 0 us -> 170 us
  matrix products: 27.1 us -> 0 us
  other arithmetic: 15.8 us -> 31.8 us
  between operations: 13.8 us -> 0.67 us
    psum x3 -> x0, waiting for transfers between devices: 354 us -> none  [the longest x1 130 us: body(): lax.psum((first_part, second_part), ('prow', 'pcol'))]
    pallas_call x0 -> x1, Pallas kernels: none -> 170 us  [body(): pl.pallas_call(functools.partial(kernel, (R, C, L, B, S, W)), out_shape=[...]
    all_gather x2 -> x0, waiting for transfers between devices: 62.3 us -> none  [one_column(): whole = lax.all_gather(masked, 'pcol', axis=1, tiled=True)]
    dot_general x4 -> x0, matrix products: 27.1 us -> none  [the longest x2 20.8 us: one_column(): jnp.einsum('lsmt,lsw->mtw', matrix, whole, precision=highest, preferred_e...]
    unnamed x2 -> x1, other arithmetic: 3.8 us -> 28.4 us
    unnamed x10 -> x11, local copies, waits for them, and re-layouts: 0.02 us -> 8.78 us
    reshape x4 -> x0, local copies, waits for them, and re-layouts: 6.25 us -> none  [the longest x2 4.77 us: one_column(): totals.reshape(row_blocks, factor, block_rows, col_width)]
  transfers between devices with their start and end apart: 5 -> 0, of which waited for: 5 -> 0; matrix products, arithmetic and copies ran while one was open for 4% -> 0% of each run, Pallas kernels for 0% -> 0%
where the time goes in v1:
time: 216 us; the launch traced here: 211 us
  Pallas kernels  170 us (79%)
  other arithmetic  31.8 us (15%)
  local copies, waits for them, and re-layouts  8.78 us (4%)
    pallas_call x1, Pallas kernels, body(): pl.pallas_call(functools.partial(kernel, (R, C, L, B, S, W)), out_shape=[...  170 us
    unnamed x1, other arithmetic  28.4 us
    unnamed x11, local copies, waits for them, and re-layouts  8.78 us

profile of v1, /device:TPU:0, one launch (start us, length us, event | category | flops | bytes accessed | tf_op | source)
XLA Modules:
  0.0 211.5 jit_solution(9133763954109058812)
XLA Ops:
  0.6 28.4 %reduce = f32[3,256,6,256]{3,2,1,0:T(8,128)} reduce(f32[3,1,256,6,1,256]{5,4,3,2,1,0:T(1,128)} %param.7, f32[]{:T(128)} %constant.3), dimensions={1,4}, to_apply=%param.7.reduce_sub_computation | reduce | bytes 9437188 | tf_op args[0]
  29.0 7.3 %copy.13 = f32[96,8,6,256]{3,1,2,0:T(8,128)} copy(f32[96,8,6,256]{3,2,1,0:T(8,128)} %bitcast.15) | data formatting | bytes 9437184
  36.3 0.0 copy-start
  36.3 0.0 copy-start.1
  36.3 170.2 %shard_map.102 = (f32[3,64,512]{2,1,0:T(8,128)}, f32[3,64,512]{2,1,0:T(8,128)}, f32[8,64,512]{2,1,0:T(8,128)}, f32[8,64,512]{2,1,0:T(8,128)}) custom-call(f32[768,1536]{1,0:T(8,128)} %bitcast.16, f32[3,2,32,512]{3,2,1,0:T(8,128)} %bitcast.19, f32[3,2,32,512]{3,2,1,0:T(8,128)} %bitcast.20, s32[24]{0:T(128)} %pat0.1, s32[24]{0:T(128)} %pat1.1), custom_call_target="tpu_custom_call" | custom-call | flops 7247757312 | bytes 4718592 | tf_op jit(solution)/shard_map/pallas_call | solution.py:317
  206.5 0.0 copy-start.3
  206.6 0.0 copy-start.2
  206.6 0.0 copy-done
  206.6 0.0 copy-done.1
  206.6 3.4 %bitcast_subtract_fusion = (f32[512,512]{1,0:T(8,128)}, f32[512,512]{1,0:T(8,128)}) fusion(f32[512,512]{1,0:T(8,128)S(1)} %copy-done, f32[8,64,512]{2,1,0:T(8,128)} %get-tuple-element.11, f32[512,512]{1,0:T(8,128)S(1)} %copy-done.1, f32[8,64,512]{2,1,0:T(8,128)} %get-tuple-element.10), kind=kLoop, calls=%fused_computation | loop fusion | flops 524288 | bytes 6291456 | tf_op jit(solution)/shard_map/sub | solution.py:365
  210.0 0.0 copy-done.3
  210.0 0.7 copy.16
  210.7 0.0 copy-done.2
  210.7 0.7 copy.17
Async XLA Ops:
  36.3 170.3 %copy-start = (f32[512,512]{1,0:T(8,128)S(1)}, f32[512,512]{1,0:T(8,128)}, u32[]{:S(2)}) copy-start(f32[512,512]{1,0:T(8,128)} %param.11) | copy-start | bytes 3145732
  36.3 170.3 %copy-start.1 = (f32[512,512]{1,0:T(8,128)S(1)}, f32[512,512]{1,0:T(8,128)}, u32[]{:S(2)}) copy-start(f32[512,512]{1,0:T(8,128)} %param.10) | copy-start | bytes 3145732
  206.5 3.4 %copy-start.3 = (f32[3,64,512]{2,1,0:T(8,128)S(1)}, f32[3,64,512]{2,1,0:T(8,128)}, u32[]{:S(2)}) copy-start(f32[3,64,512]{2,1,0:T(8,128)} %get-tuple-element.8) | copy-start | bytes 1179652
  206.6 4.2 %copy-start.2 = (f32[3,64,512]{2,1,0:T(8,128)S(1)}, f32[3,64,512]{2,1,0:T(8,128)}, u32[]{:S(2)}) copy-start(f32[3,64,512]{2,1,0:T(8,128)} %get-tuple-element.9) | copy-start | bytes 1179652

commit v2 on v1

--- a/solution.py
+++ b/solution.py
@@ -42,12 +42,14 @@
     xhi,
     xlo,
     ybuf,
-    rsbuf,
+    downbuf,
+    upbuf,
     khi,
     klo,
     chi,
     clo,
     dpart,
+    dsib,
     drecv,
     dsum,
     zbuf,
@@ -57,14 +59,22 @@
     ag_recv,
     sib_send,
     sib_recv,
-    rs_send,
-    rs_recv,
+    down_send,
+    down_recv,
+    up_send,
+    up_recv,
+    ds_send,
+    ds_recv,
     dr_send,
     dr_recv,
     dz_send,
     dz_recv,
+    dw_send,
+    dw_recv,
     da_send,
     da_recv,
+    db_send,
+    db_recv,
 ):
     R, C, L, B, S, W = sizes
     F = R // C
@@ -144,36 +154,106 @@
         part = strip(n, lax.rem(sibling + R - 2 * j, R))
         pltpu.make_async_copy(part, part, sib_recv.at[n, j]).wait()
 
-    def scatter_copy(n, d):
+    def sum_piece(n, z):
+        return ybuf.at[n, :, pl.ds(pl.multiple_of(z * S, S), S), :]
+
+    def down_copy(n, z):
+        row = lax.rem(c + C - 1, C)
+        return remote(
+            sum_piece(n, z), downbuf.at[n, z], down_send.at[n, z], down_recv.at[n, z], r, row
+        )
+
+    def up_copy(n, z):
+        row = lax.rem(c + 1, C)
+        return remote(sum_piece(n, z), upbuf.at[n, z], up_send.at[n, z], up_recv.at[n, z], r, row)
+
+    def local_wait(part, sem):
+        pltpu.make_async_copy(part, part, sem).wait()
+
+    def add_piece(n, z, buf, sem):
+        local_wait(buf.at[n, z], sem.at[n, z])
+        rows = pl.ds(pl.multiple_of(z * S, S), S)
+        for l in range(L):
+            ybuf[n, l, rows, :] = ybuf[n, l, rows, :] + buf[n, z, l]
+
+    def pass_sums(n, i):
+        @pl.when(c > i)
+        def _():
+            @pl.when(c < C - 1)
+            def _():
+                add_piece(n, i, downbuf, down_recv)
+
+            down_copy(n, i).start()
+
+        top = C - 1 - i
+
+        @pl.when(c < top)
+        def _():
+            @pl.when(c > 0)
+            def _():
+                add_piece(n, top, upbuf, up_recv)
+
+            up_copy(n, top).start()
+
+    def own_sums(n):
+        @pl.when(c < C - 1)
+        def _():
+            add_piece(n, c, downbuf, down_recv)
+
+        @pl.when(c > 0)
+        def _():
+            add_piece(n, c, upbuf, up_recv)
+
+    def chain_wait_send(n):
+        for i in range(C - 1):
+
+            @pl.when(c > i)
+            def _():
+                down_copy(n, i).wait_send()
+
+            @pl.when(c < C - 1 - i)
+            def _():
+                up_copy(n, C - 1 - i).wait_send()
+
+    def ring(j):
+        return lax.rem(r + 2 * j, R)
+
+    def diag_sib_copy(n, j):
+        k = lax.rem(sibling + 2 * j, R)
+        return remote(
+            dpart.at[n, k], dsib.at[n, j], ds_send.at[n, j], ds_recv.at[n, j], sibling, c
+        )
+
+    def diag_row_copy(n, j):
+        return remote(
+            dpart.at[n, ring(j)], drecv.at[n, j], dr_send.at[n, j], dr_recv.at[n, j], ring(j), c
+        )
+
+    def diag_piece(ref, z):
+        groups = C // lane_parts if C > lane_parts else 1
+        height = W // R // groups
+        row = pl.multiple_of(lax.div(z, C // groups) * height, height)
+        width = W // (C // groups)
+        lane = pl.multiple_of(lax.rem(z, C // groups) * width, width)
+        return ref.at[pl.ds(row, height), pl.ds(lane, width)]
+
+    def diag_col_copy(n, d):
         z = lax.rem(c + d, C)
         return remote(
-            ybuf.at[n, :, pl.ds(pl.multiple_of(z * S, S), S), :],
-            rsbuf.at[n, d],
-            rs_send.at[n, d],
-            rs_recv.at[n, d],
-            r,
-            z,
-        )
-
-    def diag_row_copy(n, d):
-        k = lax.rem(r + d, R)
-        return remote(
-            dpart.at[n, k], drecv.at[n, d], dr_send.at[n, d], dr_recv.at[n, d], k, c
-        )
-
-    def diag_col_copy(n, d):
-        return remote(
-            dsum.at[n], zbuf.at[n, d], dz_send.at[n, d], dz_recv.at[n, d], r, lax.rem(c + d, C)
-        )
-
-    def diag_all_copy(n, d):
-        return remote(
-            dias[n].at[r], dias[n].at[r], da_send.at[n, d], da_recv.at[n, d], lax.rem(r + d, R), c
-        )
-
-    def diag_all_wait(n, d):
-        part = dias[n].at[lax.rem(r + R - d, R)]
-        pltpu.make_async_copy(part, part, da_recv.at[n, d]).wait()
+            diag_piece(dsum.at[n], z), zbuf.at[n, d], dz_send.at[n, d], dz_recv.at[n, d], r, z
+        )
+
+    def diag_whole_copy(n, d):
+        part = diag_piece(dias[n].at[r], c)
+        return remote(part, part, dw_send.at[n, d], dw_recv.at[n, d], r, lax.rem(c + d, C))
+
+    def diag_all_copy(n, j):
+        part = dias[n].at[r]
+        return remote(part, part, da_send.at[n, j], da_recv.at[n, j], ring(j), c)
+
+    def diag_last_copy(n, j):
+        part = dias[n].at[lax.rem(r + R - 2 * j, R)]
+        return remote(part, part, db_send.at[n, j], db_recv.at[n, j], sibling, c)
 
     def start_first(n):
         for d in range(1, R):
@@ -220,17 +300,12 @@
                 (ahi[rows, :], alo[rows, :]), (xhi[...], xlo[...]), ((1,), (0,))
             )
 
-        for d in range(1, C):
-            scatter_copy(n, d).start()
 
     def finish_column(n):
-        for d in range(1, C):
-            scatter_copy(n, d).wait_recv()
+        own_sums(n)
         for l in range(L):
             kept = pats[n][l * R + r].astype(F32)
             value = ybuf[n, l, pl.ds(pl.multiple_of(c * S, S), S), :]
-            for d in range(1, C):
-                value = value + rsbuf[n, d, l]
             value = -(value * kept)
             cols[n][l] = value
             rows = slice(l * S, (l + 1) * S)
@@ -238,56 +313,90 @@
             khi[rows, :], klo[rows, :] = halves(panels[n][l].reshape(S, W) * kept)
         part = dot3((khi[...], klo[...]), (chi[...], clo[...]), ((0,), (0,)))
         dpart[n] = part.reshape(R, W // R, W)
-        for d in range(1, R):
-            diag_row_copy(n, d).start()
+        for j in range(R // 2):
+            diag_sib_copy(n, j).start()
 
     def diag_rows(n):
+        for j in range(R // 2):
+            diag_sib_copy(n, j).wait_recv()
+            dpart[n, ring(j)] = dpart[n, ring(j)] + dsib[n, j]
+            if j > 0:
+                diag_row_copy(n, j).start()
+
+    def diag_cols(n):
         value = dpart[n, r]
-        for d in range(1, R):
-            diag_row_copy(n, d).wait_recv()
-            value = value + drecv[n, d]
+        for j in range(1, R // 2):
+            diag_row_copy(n, j).wait_recv()
+            value = value + drecv[n, j]
         dsum[n] = value
         for d in range(1, C):
             diag_col_copy(n, d).start()
 
-    def diag_cols(n):
-        value = dsum[n]
+    def diag_whole(n):
+        value = diag_piece(dsum.at[n], c)[...]
         for d in range(1, C):
             diag_col_copy(n, d).wait_recv()
             value = value + zbuf[n, d]
-        dias[n][r] = value
-        for d in range(1, R):
-            diag_all_copy(n, d).start()
+        diag_piece(dias[n].at[r], c)[...] = value
+        for d in range(1, C):
+            diag_whole_copy(n, d).start()
+
+    def diag_all(n):
+        for d in range(1, C):
+            part = diag_piece(dias[n].at[r], lax.rem(c + C - d, C))
+            local_wait(part, dw_recv.at[n, d])
+        for j in range(1, R // 2):
+            diag_all_copy(n, j).start()
+        diag_last_copy(n, 0).start()
+
+    def diag_last(n):
+        for j in range(1, R // 2):
+            local_wait(dias[n].at[lax.rem(r + R - 2 * j, R)], da_recv.at[n, j])
+            diag_last_copy(n, j).start()
 
     start_first(0)
     start_first(1)
 
     tile = min(B, 64)
+    parts = ahi.shape[1] // LANES
 
     @pl.loop(0, L * B // tile)
     def _(i):
         rows = pl.ds(pl.multiple_of(i * tile, tile), tile)
-        ahi[rows, :], alo[rows, :] = halves(mat[rows, :])
+        for h in range(parts):
+            value = mat[pl.ds(i * tile * parts + h, tile, stride=parts), :]
+            across = slice(h * LANES, (h + 1) * LANES)
+            ahi[rows, across], alo[rows, across] = halves(value)
 
     start_gather(0)
     forward(0)
     start_gather(1)
     multiply(0)
+    pass_sums(0, 0)
     forward(1)
+    for i in range(1, C - 1):
+        pass_sums(0, i)
     multiply(1)
+    pass_sums(1, 0)
     finish_column(0)
     diag_rows(0)
+    for i in range(1, C - 1):
+        pass_sums(1, i)
+    diag_cols(0)
     finish_column(1)
-    diag_cols(0)
+    diag_whole(0)
     diag_rows(1)
+    diag_all(0)
     diag_cols(1)
+    diag_last(0)
+    diag_whole(1)
+    diag_all(1)
+    diag_last(1)
     for n in range(2):
-        for d in range(1, R):
-            diag_all_wait(n, d)
+        for j in range(R // 2):
+            local_wait(dias[n].at[lax.rem(sibling + R - 2 * j, R)], db_recv.at[n, j])
         for d in range(1, R):
             first_copy(n, d).wait_send()
-            diag_row_copy(n, d).wait_send()
-            diag_all_copy(n, d).wait_send()
 
         @pl.when(jnp.logical_not(own_plane))
         def _():
@@ -296,10 +405,15 @@
         for j in range(R // 2):
             if j > 0:
                 gather_copy(n, j).wait_send()
+                diag_row_copy(n, j).wait_send()
+                diag_all_copy(n, j).wait_send()
             sibling_copy(n, j).wait_send()
+            diag_sib_copy(n, j).wait_send()
+            diag_last_copy(n, j).wait_send()
+        chain_wait_send(n)
         for d in range(1, C):
-            scatter_copy(n, d).wait_send()
             diag_col_copy(n, d).wait_send()
+            diag_whole_copy(n, d).wait_send()
 
 
 def body(R, C, inverse, first, second, diag_first, diag_second, pat_first, pat_second):
@@ -307,12 +421,13 @@
     S, W = first.shape[2:]
     F = R // C
     RC = R // (W // LANES)
-    matrix = inverse.reshape(L * B, M * B)
+    matrix = inverse.reshape(L * B * M * B // LANES, LANES)
     panels = [p.reshape(L, RC, S // RC, W) for p in (first, second)]
     vmem = pl.BlockSpec(memory_space=pltpu.VMEM)
     smem = pl.BlockSpec(memory_space=pltpu.SMEM)
     dma = pltpu.SemaphoreType.DMA
     part = W // R
+    groups = max(1, C * LANES // W)
     flops = 3 * 2 * L * B * M * B * 2 * W
     col0, col1, sum0, sum1 = pl.pallas_call(
         functools.partial(kernel, (R, C, L, B, S, W)),
@@ -328,14 +443,16 @@
             pltpu.VMEM((M * B, W), BF16),
             pltpu.VMEM((2, L, B, W), F32),
             pltpu.VMEM((2, C, L, S, W), F32),
+            pltpu.VMEM((2, C, L, S, W), F32),
             pltpu.VMEM((L * S, W), BF16),
             pltpu.VMEM((L * S, W), BF16),
             pltpu.VMEM((L * S, W), BF16),
             pltpu.VMEM((L * S, W), BF16),
             pltpu.VMEM((2, R, part, W), F32),
-            pltpu.VMEM((2, R, part, W), F32),
+            pltpu.VMEM((2, R // 2, part, W), F32),
+            pltpu.VMEM((2, R // 2, part, W), F32),
             pltpu.VMEM((2, part, W), F32),
-            pltpu.VMEM((2, C, part, W), F32),
+            pltpu.VMEM((2, C, part // groups, W * groups // C), F32),
             dma((2, R)),
             dma((2, F * C)),
             dma((2, R // 2)),
@@ -344,12 +461,20 @@
             dma((2, R // 2)),
             dma((2, C)),
             dma((2, C)),
-            dma((2, R)),
-            dma((2, R)),
-            dma((2, C)),
-            dma((2, C)),
-            dma((2, R)),
-            dma((2, R)),
+            dma((2, C)),
+            dma((2, C)),
+            dma((2, R // 2)),
+            dma((2, R // 2)),
+            dma((2, R // 2)),
+            dma((2, R // 2)),
+            dma((2, C)),
+            dma((2, C)),
+            dma((2, C)),
+            dma((2, C)),
+            dma((2, R // 2)),
+            dma((2, R // 2)),
+            dma((2, R // 2)),
+            dma((2, R // 2)),
         ],
         compiler_params=pltpu.CompilerParams(
             collective_id=0, has_side_effects=True, vmem_limit_bytes=56 * 1024 * 1024

time: 216 us -> 173 us (0.80); the launches traced: 211 us -> 172 us
  other arithmetic: 31.8 us -> 3.4 us
  local copies, waits for them, and re-layouts: 8.78 us -> 1.51 us
  Pallas kernels: 170 us -> 167 us
    unnamed x1 -> x0, other arithmetic: 28.4 us -> none
    unnamed x11 -> x10, local copies, waits for them, and re-layouts: 8.78 us -> 1.51 us
    pallas_call x1, Pallas kernels: 170 us -> 167 us  [body(): pl.pallas_call(functools.partial(kernel, (R, C, L, B, S, W)), out_shape=[...]
where the time goes in v2:
time: 173 us; the launch traced here: 172 us
  Pallas kernels  167 us (97%)
  other arithmetic  3.4 us (2%)
    pallas_call x1, Pallas kernels, body(): pl.pallas_call(functools.partial(kernel, (R, C, L, B, S, W)), out_shape=[...  167 us

profile of v2, /device:TPU:0, one launch (start us, length us, event | category | flops | bytes accessed | tf_op | source)
XLA Modules:
  0.0 172.5 jit_solution(1765049772294378513)
XLA Ops:
  0.6 0.0 copy-start
  0.6 0.0 copy-start.1
  0.7 166.9 %shard_map.102 = (f32[3,64,512]{2,1,0:T(8,128)}, f32[3,64,512]{2,1,0:T(8,128)}, f32[8,64,512]{2,1,0:T(8,128)}, f32[8,64,512]{2,1,0:T(8,128)}) custom-call(f32[9216,128]{1,0:T(8,128)} %bitcast.15, f32[3,2,32,512]{3,2,1,0:T(8,128)} %bitcast.16, f32[3,2,32,512]{3,2,1,0:T(8,128)} %bitcast.17, s32[24]{0:T(128)} %pat0.1, s32[24]{0:T(128)} %pat1.1), custom_call_target="tpu_custom_call" | custom-call | flops 7247757312 | bytes 4718592 | tf_op jit(solution)/shard_map/pallas_call | solution.py:432
  167.5 0.0 copy-start.3
  167.5 0.0 copy-start.2
  167.5 0.0 copy-done
  167.5 0.0 copy-done.1
  167.6 3.4 %bitcast_subtract_fusion = (f32[512,512]{1,0:T(8,128)}, f32[512,512]{1,0:T(8,128)}) fusion(f32[512,512]{1,0:T(8,128)S(1)} %copy-done, f32[8,64,512]{2,1,0:T(8,128)} %get-tuple-element.11, f32[512,512]{1,0:T(8,128)S(1)} %copy-done.1, f32[8,64,512]{2,1,0:T(8,128)} %get-tuple-element.10), kind=kLoop, calls=%fused_computation | loop fusion | flops 524288 | bytes 6291456 | tf_op jit(solution)/shard_map/sub | solution.py:490
  171.0 0.0 copy-done.3
  171.0 0.7 copy.15
  171.7 0.0 copy-done.2
  171.7 0.7 copy.16
Async XLA Ops:
  0.6 166.9 %copy-start = (f32[512,512]{1,0:T(8,128)S(1)}, f32[512,512]{1,0:T(8,128)}, u32[]{:S(2)}) copy-start(f32[512,512]{1,0:T(8,128)} %param.11) | copy-start | bytes 3145732
  0.6 166.9 %copy-start.1 = (f32[512,512]{1,0:T(8,128)S(1)}, f32[512,512]{1,0:T(8,128)}, u32[]{:S(2)}) copy-start(f32[512,512]{1,0:T(8,128)} %param.10) | copy-start | bytes 3145732
  167.5 3.4 %copy-start.3 = (f32[3,64,512]{2,1,0:T(8,128)S(1)}, f32[3,64,512]{2,1,0:T(8,128)}, u32[]{:S(2)}) copy-start(f32[3,64,512]{2,1,0:T(8,128)} %get-tuple-element.8) | copy-start | bytes 1179652
  167.5 4.2 %copy-start.2 = (f32[3,64,512]{2,1,0:T(8,128)S(1)}, f32[3,64,512]{2,1,0:T(8,128)}, u32[]{:S(2)}) copy-start(f32[3,64,512]{2,1,0:T(8,128)} %get-tuple-element.9) | copy-start | bytes 1179652

commit v3 on v2

--- a/solution.py
+++ b/solution.py
@@ -42,8 +42,7 @@
     xhi,
     xlo,
     ybuf,
-    downbuf,
-    upbuf,
+    rsbuf,
     khi,
     klo,
     chi,
@@ -59,10 +58,8 @@
     ag_recv,
     sib_send,
     sib_recv,
-    down_send,
-    down_recv,
-    up_send,
-    up_recv,
+    rs_send,
+    rs_recv,
     ds_send,
     ds_recv,
     dr_send,
@@ -121,20 +118,20 @@
     def first_copy(n, d):
         k = lax.rem(r + d, R)
         src = panels[n].at[:, row_part(k), :, lanes(k)]
-        dst = xbuf.at[n, :, source, row_part(k), :, lanes(k)]
+        dst = xbuf.at[n, k, :, source]
         return remote(src, dst, s1_send.at[n, d], s1_recv.at[n, source], k, plane)
 
     def first_local(n):
         src = panels[n].at[:, row_part(r), :, lanes(r)]
-        dst = xbuf.at[n, :, source, row_part(r), :, lanes(r)]
+        dst = xbuf.at[n, r, :, source]
         return pltpu.make_async_copy(src, dst, s1_recv.at[n, source])
 
     def first_wait(n, q):
-        part = xbuf.at[n, :, q, row_part(r), :, lanes(r)]
+        part = xbuf.at[n, r, :, q]
         pltpu.make_async_copy(part, part, s1_recv.at[n, q]).wait()
 
     def strip(n, k):
-        return xbuf.at[n, :, :, row_part(k), :, lanes(k)]
+        return xbuf.at[n, k]
 
     def gather_copy(n, j):
         part = strip(n, r)
@@ -154,66 +151,19 @@
         part = strip(n, lax.rem(sibling + R - 2 * j, R))
         pltpu.make_async_copy(part, part, sib_recv.at[n, j]).wait()
 
-    def sum_piece(n, z):
-        return ybuf.at[n, :, pl.ds(pl.multiple_of(z * S, S), S), :]
-
-    def down_copy(n, z):
-        row = lax.rem(c + C - 1, C)
+    def scatter_copy(n, d):
+        z = lax.rem(c + d, C)
         return remote(
-            sum_piece(n, z), downbuf.at[n, z], down_send.at[n, z], down_recv.at[n, z], r, row
-        )
-
-    def up_copy(n, z):
-        row = lax.rem(c + 1, C)
-        return remote(sum_piece(n, z), upbuf.at[n, z], up_send.at[n, z], up_recv.at[n, z], r, row)
+            ybuf.at[n, :, pl.ds(pl.multiple_of(z * S, S), S), :],
+            rsbuf.at[n, d],
+            rs_send.at[n, d],
+            rs_recv.at[n, d],
+            r,
+            z,
+        )
 
     def local_wait(part, sem):
         pltpu.make_async_copy(part, part, sem).wait()
-
-    def add_piece(n, z, buf, sem):
-        local_wait(buf.at[n, z], sem.at[n, z])
-        rows = pl.ds(pl.multiple_of(z * S, S), S)
-        for l in range(L):
-            ybuf[n, l, rows, :] = ybuf[n, l, rows, :] + buf[n, z, l]
-
-    def pass_sums(n, i):
-        @pl.when(c > i)
-        def _():
-            @pl.when(c < C - 1)
-            def _():
-                add_piece(n, i, downbuf, down_recv)
-
-            down_copy(n, i).start()
-
-        top = C - 1 - i
-
-        @pl.when(c < top)
-        def _():
-            @pl.when(c > 0)
-            def _():
-                add_piece(n, top, upbuf, up_recv)
-
-            up_copy(n, top).start()
-
-    def own_sums(n):
-        @pl.when(c < C - 1)
-        def _():
-            add_piece(n, c, downbuf, down_recv)
-
-        @pl.when(c > 0)
-        def _():
-            add_piece(n, c, upbuf, up_recv)
-
-    def chain_wait_send(n):
-        for i in range(C - 1):
-
-            @pl.when(c > i)
-            def _():
-                down_copy(n, i).wait_send()
-
-            @pl.when(c < C - 1 - i)
-            def _():
-                up_copy(n, C - 1 - i).wait_send()
 
     def ring(j):
         return lax.rem(r + 2 * j, R)
@@ -288,10 +238,14 @@
             l = lax.div(i, F * C)
             q = lax.rem(i, F * C)
             kept = pats[n][l * R + lax.div(q, C) * C + c].astype(F32)
+            bands = [
+                jnp.concatenate(
+                    [xbuf[n, g * lane_parts + h, l, q] for h in range(lane_parts)], axis=1
+                )
+                for g in range(RC)
+            ]
             rows = pl.ds(pl.multiple_of(i * S, S), S)
-            high, low = halves(xbuf[n, l, q].reshape(S, W) * kept)
-            xhi[rows, :] = high
-            xlo[rows, :] = low
+            xhi[rows, :], xlo[rows, :] = halves(jnp.concatenate(bands, axis=0) * kept)
 
         @pl.loop(0, L)
         def _(l):
@@ -301,11 +255,18 @@
             )
 
 
+    def scatter(n):
+        for d in range(1, C):
+            scatter_copy(n, d).start()
+
     def finish_column(n):
-        own_sums(n)
+        for d in range(1, C):
+            scatter_copy(n, d).wait_recv()
         for l in range(L):
             kept = pats[n][l * R + r].astype(F32)
             value = ybuf[n, l, pl.ds(pl.multiple_of(c * S, S), S), :]
+            for d in range(1, C):
+                value = value + rsbuf[n, d, l]
             value = -(value * kept)
             cols[n][l] = value
             rows = slice(l * S, (l + 1) * S)
@@ -355,6 +316,7 @@
             diag_last_copy(n, j).start()
 
     start_first(0)
+    start_gather(0)
     start_first(1)
 
     tile = min(B, 64)
@@ -368,27 +330,22 @@
             across = slice(h * LANES, (h + 1) * LANES)
             ahi[rows, across], alo[rows, across] = halves(value)
 
-    start_gather(0)
     forward(0)
     start_gather(1)
     multiply(0)
-    pass_sums(0, 0)
+    scatter(0)
     forward(1)
-    for i in range(1, C - 1):
-        pass_sums(0, i)
     multiply(1)
-    pass_sums(1, 0)
+    scatter(1)
     finish_column(0)
     diag_rows(0)
-    for i in range(1, C - 1):
-        pass_sums(1, i)
     diag_cols(0)
+    diag_whole(0)
     finish_column(1)
-    diag_whole(0)
+    diag_all(0)
     diag_rows(1)
-    diag_all(0)
+    diag_last(0)
     diag_cols(1)
-    diag_last(0)
     diag_whole(1)
     diag_all(1)
     diag_last(1)
@@ -410,8 +367,8 @@
             sibling_copy(n, j).wait_send()
             diag_sib_copy(n, j).wait_send()
             diag_last_copy(n, j).wait_send()
-        chain_wait_send(n)
-        for d in range(1, C):
+        for d in range(1, C):
+            scatter_copy(n, d).wait_send()
             diag_col_copy(n, d).wait_send()
             diag_whole_copy(n, d).wait_send()
 
@@ -436,13 +393,12 @@
         in_specs=[vmem] * 3 + [smem] * 2,
         out_specs=[vmem] * 4,
         scratch_shapes=[
-            pltpu.VMEM((2, L, F * C, RC, S // RC, W), F32),
+            pltpu.VMEM((2, R, L, F * C, S // RC, LANES), F32),
             pltpu.VMEM((L * B, M * B), BF16),
             pltpu.VMEM((L * B, M * B), BF16),
             pltpu.VMEM((M * B, W), BF16),
             pltpu.VMEM((M * B, W), BF16),
             pltpu.VMEM((2, L, B, W), F32),
-            pltpu.VMEM((2, C, L, S, W), F32),
             pltpu.VMEM((2, C, L, S, W), F32),
             pltpu.VMEM((L * S, W), BF16),
             pltpu.VMEM((L * S, W), BF16),
@@ -459,8 +415,6 @@
             dma((2, R // 2)),
             dma((2, R // 2)),
             dma((2, R // 2)),
-            dma((2, C)),
-            dma((2, C)),
             dma((2, C)),
             dma((2, C)),
             dma((2, R // 2)),

time: 173 us -> 174 us (level)
  no operation moved by 1% of the time
where the time goes in v3:
time: 174 us
  Pallas kernels  168 us (97%)
  other arithmetic  3.4 us (2%)
    pallas_call x1, Pallas kernels, body(): pl.pallas_call(functools.partial(kernel, (R, C, L, B, S, W)), out_shape=[...  168 us

profile of v3, /device:TPU:0, one launch (start us, length us, event | category | flops | bytes accessed | tf_op | source)
XLA Modules:
  0.0 173.8 jit_solution(7249770551154308481)
XLA Ops:
  0.6 0.0 copy-start
  0.6 0.0 copy-start.1
  0.7 168.2 %shard_map.102 = (f32[3,64,512]{2,1,0:T(8,128)}, f32[3,64,512]{2,1,0:T(8,128)}, f32[8,64,512]{2,1,0:T(8,128)}, f32[8,64,512]{2,1,0:T(8,128)}) custom-call(f32[9216,128]{1,0:T(8,128)} %bitcast.15, f32[3,2,32,512]{3,2,1,0:T(8,128)} %bitcast.16, f32[3,2,32,512]{3,2,1,0:T(8,128)} %bitcast.17, s32[24]{0:T(128)} %pat0.1, s32[24]{0:T(128)} %pat1.1), custom_call_target="tpu_custom_call" | custom-call | flops 7247757312 | bytes 4718592 | tf_op jit(solution)/shard_map/pallas_call | solution.py:389
  168.9 0.0 copy-start.3
  168.9 0.0 copy-start.2
  168.9 0.0 copy-done
  168.9 0.0 copy-done.1
  168.9 3.4 %bitcast_subtract_fusion = (f32[512,512]{1,0:T(8,128)}, f32[512,512]{1,0:T(8,128)}) fusion(f32[512,512]{1,0:T(8,128)S(1)} %copy-done, f32[8,64,512]{2,1,0:T(8,128)} %get-tuple-element.11, f32[512,512]{1,0:T(8,128)S(1)} %copy-done.1, f32[8,64,512]{2,1,0:T(8,128)} %get-tuple-element.10), kind=kLoop, calls=%fused_computation | loop fusion | flops 524288 | bytes 6291456 | tf_op jit(solution)/shard_map/sub | solution.py:444
  172.3 0.0 copy-done.3
  172.4 0.7 copy.15
  173.1 0.0 copy-done.2
  173.1 0.7 copy.16
Async XLA Ops:
  0.6 168.3 %copy-start = (f32[512,512]{1,0:T(8,128)S(1)}, f32[512,512]{1,0:T(8,128)}, u32[]{:S(2)}) copy-start(f32[512,512]{1,0:T(8,128)} %param.11) | copy-start | bytes 3145732
  0.6 168.3 %copy-start.1 = (f32[512,512]{1,0:T(8,128)S(1)}, f32[512,512]{1,0:T(8,128)}, u32[]{:S(2)}) copy-start(f32[512,512]{1,0:T(8,128)} %param.10) | copy-start | bytes 3145732
  168.9 3.4 %copy-start.3 = (f32[3,64,512]{2,1,0:T(8,128)S(1)}, f32[3,64,512]{2,1,0:T(8,128)}, u32[]{:S(2)}) copy-start(f32[3,64,512]{2,1,0:T(8,128)} %get-tuple-element.8) | copy-start | bytes 1179652
  168.9 4.2 %copy-start.2 = (f32[3,64,512]{2,1,0:T(8,128)S(1)}, f32[3,64,512]{2,1,0:T(8,128)}, u32[]{:S(2)}) copy-start(f32[3,64,512]{2,1,0:T(8,128)} %get-tuple-element.9) | copy-start | bytes 1179652
